TPU v7x, 512 devices: a whole 4x4x16 slice. The times are simulated.
512 devices in a mesh: ens: 8 (over y_lo, x), slab: 64 (over y_hi, z, core).
Axes of the slice: x: 4, y: 4 (y_hi: 2, y_lo: 2; y = y_hi * 2 + y_lo), z: 16, core: 2. Of those that a mesh axis runs over, the one named last changes fastest.
Arguments:
- state: float32 [64, 64, 1024], P('slab'), may hold values from -6 to 6
- face_coefs: bfloat16 [2, 64, 64, 1024], P(None, 'slab'), may hold values from 0.019897461 to 0.19921875
- codes: int32 [8], P('ens'), may hold values from 0 to 999999
- acoustic_inv: float32 [64, 64, 64], P('slab')
- bounds: int32 [5], replicated, may hold values from 0 to 64, as said below
- land_mask: int32 [64, 1024], P('slab'), may hold values 0 or 1
- target: bfloat16 [64, 64, 1024], P(None, 'slab'), may hold values from -6 to 6
- w_in: bfloat16 [64, 1024], replicated, may hold values from -0.75 to 0.75
- bias_in: float32 [1024], replicated, may hold values from -3 to 3
- land_weight: float32 [1024], replicated, may hold values from -4 to 4
- w_out: bfloat16 [1024, 64], replicated, may hold values from -0.1875 to 0.1875
- bias_out: float32 [64], replicated, may hold values from -3 to 3
Outputs:
- upd_in: float32 [64, 1024], replicated
- upd_out: float32 [1024, 64], replicated
- grad_state: float32 [64, 64, 1024], P('slab')
Inputs may be any that keep to these rules, and one draw needn't show every extreme that they name: bounds[0] = 0 and bounds[4] = 64; the entries rise strictly.
All inputs are finite; a program needn't handle non-finite values. No bound on the sum of `land_mask` on one device may be relied on, other than what follows from the above.
Results may differ from a plain program's by a relative error of at most 0.0004.
The roundings to bfloat16 on the way count: a program that leaves them out, or rounds other values in their place, can miss the bound.
Values sent between devices are 32-bit elements; how exact they have to be, the bound alone decides.
A program may use at most 64 MiB of HBM per device.

v0:
```python
import jax
import jax.numpy as jnp
from jax import lax
from jax.sharding import PartitionSpec as P


def noise(code, cell):
    mult = code % 251 + 2
    first = (mult * (cell % 65521) + 12345) % 65521
    second = (first * 31337 + mult) % 65521
    return second.astype(jnp.float32) / 65521.0 - 0.5


def diffuse(field, east, north):
    flux_x = east * (jnp.roll(field, -1, axis=2) - field)
    step_y = jnp.concatenate([field[:, 1:] - field[:, :-1], jnp.zeros_like(field[:, :1])], axis=1)
    flux_y = north * step_y
    lower = jnp.concatenate([jnp.zeros_like(flux_y[:, :1]), flux_y[:, :-1]], axis=1)
    return field + flux_x - jnp.roll(flux_x, 1, axis=2) + flux_y - lower


def column_step(
    x_row, land_row, target_row, solve_row, w_in, bias_in, land_weight, w_out, bias_out, scale
):
    pre = lax.dot_general(w_in, x_row, (((0,), (0,)), ((), ())), preferred_element_type=jnp.float32)
    pre = pre + bias_in[:, None] + land_weight[:, None] * land_row[None, :]
    sig = jax.nn.sigmoid(pre)
    hidden = (pre * sig).astype(jnp.bfloat16)
    out = lax.dot_general(
        w_out, hidden, (((0,), (0,)), ((), ())), preferred_element_type=jnp.float32
    )
    out = out + bias_out[:, None]
    d_out = ((out - target_row.astype(jnp.float32)) * scale).astype(jnp.bfloat16)
    g_out = lax.dot_general(
        hidden, d_out, (((1,), (1,)), ((), ())), preferred_element_type=jnp.float32
    )
    d_hidden = jnp.dot(w_out, d_out, preferred_element_type=jnp.float32)
    d_pre = (d_hidden * sig * (1.0 + pre * (1.0 - sig))).astype(jnp.bfloat16)
    g_in = lax.dot_general(
        x_row, d_pre, (((1,), (1,)), ((), ())), preferred_element_type=jnp.float32
    )
    d_x = jnp.dot(w_in, d_pre, preferred_element_type=jnp.float32)
    d_h = lax.dot_general(solve_row, d_x, (((0,), (0,)), ((), ())), precision=lax.Precision.HIGHEST)
    return (g_in, g_out, d_h)


def normalized(grad):
    return grad / jnp.sqrt(jnp.mean(grad * grad) + 1e-06)


def on_device(
    state,
    face_coefs,
    codes,
    acoustic_inv,
    bounds,
    land_mask,
    target,
    w_in,
    bias_in,
    land_weight,
    w_out,
    bias_out,
):
    lev_local, lat_count, lon_count = state.shape
    level_count = w_in.shape[0]
    hidden_count = w_in.shape[1]
    lat_local = land_mask.shape[0]
    block_count = bounds.shape[0] - 1
    east = face_coefs[0].astype(jnp.float32)
    north = face_coefs[1].astype(jnp.float32)
    first_level = lax.axis_index("slab") * lev_local
    level_ids = first_level + jnp.arange(lev_local, dtype=jnp.int32)
    lat_ids = jnp.arange(lat_count, dtype=jnp.int32)
    lon_ids = jnp.arange(lon_count, dtype=jnp.int32)
    cell = (level_ids[:, None, None] * lat_count + lat_ids[None, :, None]) * lon_count + lon_ids[
        None, None, :
    ]
    fresh = diffuse(state + noise(codes[0], cell), east, north)
    columns = lax.all_to_all(fresh, "slab", split_axis=1, concat_axis=0, tiled=True)
    level = jnp.arange(level_count, dtype=jnp.int32)
    block = jnp.sum((level[:, None] >= bounds[None, 1:block_count]).astype(jnp.int32), axis=1)
    couple = (block[:, None] == block[None, :]).astype(jnp.float32)
    solve_mat = acoustic_inv * couple[None]
    land = land_mask.astype(jnp.float32)
    scale = 1.0 / lax.axis_size("ens")

    def per_row(row, carry):
        acc_in, acc_out, back = carry
        source = lax.dynamic_index_in_dim(columns, row, 1, keepdims=False)
        solve_row = lax.dynamic_index_in_dim(solve_mat, row, 0, keepdims=False)
        x_row = jnp.dot(solve_row, source, precision=lax.Precision.HIGHEST).astype(jnp.bfloat16)
        land_row = lax.dynamic_index_in_dim(land, row, 0, keepdims=False)
        target_row = lax.dynamic_index_in_dim(target, row, 1, keepdims=False)
        part_in, part_out, d_h = column_step(
            x_row,
            land_row,
            target_row,
            solve_row,
            w_in,
            bias_in,
            land_weight,
            w_out,
            bias_out,
            scale,
        )
        back = d_h[:, None, :]
        return (acc_in + part_in, acc_out + part_out, back)

    start = (
        jnp.zeros((level_count, hidden_count), jnp.float32),
        jnp.zeros((hidden_count, level_count), jnp.float32),
        jnp.zeros((level_count, lat_local, lon_count), jnp.float32),
    )
    g_in, g_out, back = lax.fori_loop(0, lat_local, per_row, start)
    g_in, g_out = lax.psum((g_in, g_out), ("ens", "slab"))
    returned = lax.all_to_all(back, "slab", split_axis=0, concat_axis=1, tiled=True)
    summed = lax.psum(returned, "ens")
    grad_state = diffuse(summed, east, north)
    return (normalized(g_in), normalized(g_out), grad_state)


def solution(mesh):
    placed = (
        P("slab", None, None),
        P(None, "slab", None, None),
        P("ens"),
        P("slab", None, None),
        P(),
        P("slab", None),
        P(None, "slab", None),
        P(),
        P(),
        P(),
        P(),
        P(),
    )
    return jax.shard_map(
        on_device,
        mesh=mesh,
        in_specs=placed,
        out_specs=(P(), P(), P("slab", None, None)),
        check_vma=False,
    )
```

profile of v0, /device:TPU:32, one launch (start us, length us, event | category | flops | bytes accessed | tf_op | source)
XLA Modules:
  0.0 652.6 jit_solution(9690819280671128844)
XLA Ops:
  8.8 4.9 fusion.15
  13.9 0.6 slice.72
  14.5 1.0 fusion.36
  15.5 5.8 fusion.16
  21.5 5.2 fusion.18
  26.7 18.4 %all-to-all-start = ((f32[1,64,1024]{2,0,1:T(1,128)}), f32[1,64,1024]{2,0,1:T(1,128)S(1)}, u32[]{:S(2)}, u32[]{:S(2)}) async-start(f32[1,64,1024]{2,0,1:T(1,128)} %fusion.18), calls=%async_computation | async-start | bytes 524288 | tf_op jit(solution)/shard_map/all_to_all | solution.py:80
  45.3 22.7 %all-to-all-done = f32[1,64,1024]{2,0,1:T(1,128)S(1)} async-done(((f32[1,64,1024]{2,0,1:T(1,128)}), f32[1,64,1024]{2,0,1:T(1,128)S(1)}, u32[]{:S(2)}, u32[]{:S(2)}) %all-to-all-start) | async-done | bytes 262176 | tf_op jit(solution)/shard_map/all_to_all | solution.py:80
  68.0 0.4 convolution_convert_fusion
  68.5 1.4 multiply_convert_fusion
  69.9 0.8 fusion.5
  70.7 0.5 copy-done.1
  71.2 2.1 fusion.1
  73.4 0.8 fusion.38
  74.1 0.5 convolution_bitcast_fusion
  74.6 1.0 copy.23
  75.6 4.9 all-to-all-start.1
  80.5 2.8 fusion.39
  83.3 1.2 fusion.37
  84.7 459.8 %all-reduce.10.cloned.1.call-done = (f32[64,1024]{1,0:T(8,128)}, f32[1024,64]{0,1:T(8,128)}) async-done(((f32[64,1024]{1,0:T(8,128)}, f32[1024,64]{0,1:T(8,128)}), (f32[64,1024]{1,0:T(8,128)}, f32[1024,64]{0,1:T(8,128)})) %all-reduce.10.cloned.1.call-update) | async-done | bytes 524304 | tf_op jit(solution)/shard_map/psum | solution.py:116
  544.6 1.6 multiply_reduce_fusion.1
  546.9 1.7 broadcast_divide_fusion.1
  548.6 0.7 copy-done.3
  549.3 1.6 multiply_reduce_fusion
  551.6 1.7 broadcast_divide_fusion
  553.3 83.9 %all-reduce.8.cloned.1.call-done = f32[1,64,1024]{2,0,1:T(1,128)} async-done(((f32[1,64,1024]{2,0,1:T(1,128)}), f32[1,64,1024]{2,0,1:T(1,128)}) %all-reduce.8.cloned.1.call-update) | async-done | bytes 262160 | tf_op jit(solution)/shard_map/psum | solution.py:118
  637.2 1.3 slice_subtract_fusion
  638.6 0.3 pad_multiply_fusion
  638.9 0.8 slice.80
  639.6 1.6 slice.79
  641.2 1.4 fusion.19
  642.7 1.7 fusion.21
  644.4 0.8 copy.24
  (37 shorter events, 1.0 us)
Async XLA Ops:
  8.0 60.4 %copy-start = (bf16[64,1024]{1,0:T(8,128)(2,1)S(1)}, bf16[64,1024]{1,0:T(8,128)(2,1)}, u32[]{:S(2)}) copy-start(bf16[64,1024]{1,0:T(8,128)(2,1)} %param.19) | copy-start | bytes 393220
  8.0 13.5 %copy-start.2 = (f32[1,64,1024]{2,1,0:T(8,128)S(1)}, f32[1,64,1024]{2,1,0:T(8,128)}, u32[]{:S(2)}) copy-start(f32[1,64,1024]{2,1,0:T(8,128)} %param.12) | copy-start | bytes 786436
  8.0 37.1 %copy-start.11 = (s32[5]{0:T(128)S(1)}, s32[5]{0:T(128)}, u32[]{:S(2)}) copy-start(s32[5]{0:T(128)} %param.16) | copy-start | bytes 64
  8.0 37.1 %copy-start.7 = (s32[1,1024]{1,0:T(1,128)S(1)}, s32[1,1024]{1,0:T(1,128)}, u32[]{:S(2)}) copy-start(s32[1,1024]{1,0:T(1,128)} %param.17) | copy-start | bytes 12292
  8.0 59.9 %copy-start.4 = (f32[1,64,64]{2,1,0:T(8,128)S(1)}, f32[1,64,64]{2,1,0:T(8,128)}, u32[]{:S(2)}) copy-start(f32[1,64,64]{2,1,0:T(8,128)} %param.15) | copy-start | bytes 49156
  8.1 60.3 %copy-start.9 = (f32[1024]{0:T(1024)S(1)}, f32[1024]{0:T(1024)}, u32[]{:S(2)}) copy-start(f32[1024]{0:T(1024)} %param.21) | copy-start | bytes 12292
  8.1 60.3 %copy-start.10 = (f32[1024]{0:T(1024)S(1)}, f32[1024]{0:T(1024)}, u32[]{:S(2)}) copy-start(f32[1024]{0:T(1024)} %param.20) | copy-start | bytes 12292
  26.7 41.3 %all-to-all-start = ((f32[1,64,1024]{2,0,1:T(1,128)}), f32[1,64,1024]{2,0,1:T(1,128)S(1)}, u32[]{:S(2)}, u32[]{:S(2)}) async-start(f32[1,64,1024]{2,0,1:T(1,128)} %fusion.18), calls=%async_computation | async-start | bytes 524288 | tf_op jit(solution)/shard_map/all_to_all | solution.py:80
  68.4 1.5 copy-start.5
  68.4 1.5 copy-start.6
  68.4 1.5 copy-start.8
  69.9 1.3 copy-start.1
  75.6 473.0 %all-to-all-start.1 = ((f32[64,1,1024]{2,1,0:T(1,128)}), f32[64,1,1024]{2,1,0:T(1,128)S(1)}, u32[]{:S(2)}, u32[]{:S(2)}) async-start(f32[64,1,1024]{2,1,0:T(1,128)} %copy.23), calls=%async_computation.1 | async-start | bytes 524288 | tf_op jit(solution)/shard_map/all_to_all | solution.py:117
  80.5 464.1 %all-reduce.10.cloned.1.call-start = ((), (), s32[]{:S(2)}) async-start(), calls=%async_computation.3 | async-start | bytes 1048576 | tf_op jit(solution)/shard_map/psum | solution.py:116
  84.5 552.7 %all-reduce.8.cloned.1.call-start = ((), (), s32[]{:S(2)}) async-start(), calls=%async_computation.2 | async-start | bytes 524288 | tf_op jit(solution)/shard_map/psum | solution.py:118
  548.6 0.7 copy-start.3
Sparse Core Ops, SparseCore 0:
  87.4 457.1 all-reduce.9
Sparse Core Ops, SparseCore 1:
  549.4 87.8 all-reduce.7
where the time goes:
time: 653 us
  waiting for transfers between devices  567 us (87%)
  other arithmetic  27.4 us (4%)
  starting transfers between devices  23.5 us (4%)
  between operations  17.9 us (3%)
  matrix products  9.94 us (2%)
  local copies, waits for them, and re-layouts  7.28 us (1%)
    psum x1, waiting for transfers between devices, on_device(): g_in, g_out = lax.psum((g_in, g_out), ('ens', 'slab'))  460 us
    psum x1, waiting for transfers between devices, on_device(): summed = lax.psum(returned, 'ens')  83.9 us
    all_to_all x1, waiting for transfers between devices, on_device(): lax.all_to_all(fresh, 'slab', split_axis=1, concat_axis=0, tiled=True)  22.7 us
    all_to_all x1, starting transfers between devices, on_device(): lax.all_to_all(fresh, 'slab', split_axis=1, concat_axis=0, tiled=True)  18.4 us
  transfers between devices with their start and end apart: 4, of which 3 were waited for; matrix products, arithmetic and copies ran while one was open for 2% of the time, Pallas kernels for 0%

commit v1 on v0

--- a/solution.py
+++ b/solution.py
@@ -113,7 +113,7 @@
         jnp.zeros((level_count, lat_local, lon_count), jnp.float32),
     )
     g_in, g_out, back = lax.fori_loop(0, lat_local, per_row, start)
-    g_in, g_out = lax.psum((g_in, g_out), ("ens", "slab"))
+    g_in, g_out = lax.psum(lax.psum((g_in, g_out), axis_name="slab"), "ens")
     returned = lax.all_to_all(back, "slab", split_axis=0, concat_axis=1, tiled=True)
     summed = lax.psum(returned, "ens")
     grad_state = diffuse(summed, east, north)

time: 653 us -> 714 us (1.093)
  waiting for transfers between devices: 567 us -> 630 us
    psum x2, waiting for transfers between devices: 544 us -> 607 us  [on_device(): g_in, g_out = lax.psum(lax.psum((g_in, g_out), axis_name='slab'), 'ens')]
  transfers between devices with their start and end apart: 4 -> 4, of which waited for: 3 -> 3; matrix products, arithmetic and copies ran while one was open for 2% -> 1% of each run, Pallas kernels for 0% -> 0%
where the time goes in v1:
time: 714 us; the launch traced here: 713 us
  waiting for transfers between devices  630 us (88%)
  other arithmetic  25.5 us (4%)
  starting transfers between devices  23.5 us (3%)
  between operations  16.5 us (2%)
  matrix products  9.95 us (1%)
  local copies, waits for them, and re-layouts  7.38 us (1%)
    psum x2, waiting for transfers between devices, on_device(): g_in, g_out = lax.psum(lax.psum((g_in, g_out), axis_name='slab'), 'ens')  607 us
    all_to_all x1, waiting for transfers between devices, on_device(): lax.all_to_all(fresh, 'slab', split_axis=1, concat_axis=0, tiled=True)  22.7 us
    all_to_all x1, starting transfers between devices, on_device(): lax.all_to_all(fresh, 'slab', split_axis=1, concat_axis=0, tiled=True)  18.4 us
  transfers between devices with their start and end apart: 4, of which 3 were waited for; matrix products, arithmetic and copies ran while one was open for 1% of the time, Pallas kernels for 0%

profile of v1, /device:TPU:32, one launch (start us, length us, event | category | flops | bytes accessed | tf_op | source)
XLA Modules:
  0.0 713.1 jit_solution(2908997914553234175)
XLA Ops:
  8.0 4.9 fusion.15
  13.1 0.6 slice.72
  13.7 1.0 fusion.36
  14.7 5.8 fusion.16
  20.7 5.2 fusion.18
  25.9 18.4 %all-to-all-start = ((f32[1,64,1024]{2,0,1:T(1,128)}), f32[1,64,1024]{2,0,1:T(1,128)S(1)}, u32[]{:S(2)}, u32[]{:S(2)}) async-start(f32[1,64,1024]{2,0,1:T(1,128)} %fusion.18), calls=%async_computation | async-start | bytes 524288 | tf_op jit(solution)/shard_map/all_to_all | solution.py:80
  44.4 22.7 %all-to-all-done = f32[1,64,1024]{2,0,1:T(1,128)S(1)} async-done(((f32[1,64,1024]{2,0,1:T(1,128)}), f32[1,64,1024]{2,0,1:T(1,128)S(1)}, u32[]{:S(2)}, u32[]{:S(2)}) %all-to-all-start) | async-done | bytes 262176 | tf_op jit(solution)/shard_map/all_to_all | solution.py:80
  67.1 0.4 convolution_convert_fusion
  67.6 1.4 multiply_convert_fusion
  69.1 0.8 fusion.5
  69.9 0.5 copy-done.1
  70.4 2.1 fusion.1
  72.5 0.8 fusion.38
  73.3 0.5 convolution_bitcast_fusion
  73.8 1.0 copy.23
  74.8 4.9 all-to-all-start.1
  79.7 2.8 fusion.39
  82.5 1.2 fusion.37
  83.9 518.7 %all-reduce.9.cloned.1.call-done = (f32[64,1024]{1,0:T(8,128)}, f32[1024,64]{0,1:T(8,128)}) async-done(((f32[64,1024]{1,0:T(8,128)}, f32[1024,64]{0,1:T(8,128)}), (f32[64,1024]{1,0:T(8,128)}, f32[1024,64]{0,1:T(8,128)})) %all-reduce.9.cloned.1.call-update) | async-done | bytes 524304 | tf_op jit(solution)/shard_map/psum | solution.py:116
  602.6 0.7 copy-done.4
  603.3 88.8 %all-reduce.11.cloned.1.call-done = (f32[64,1024]{1,0:T(8,128)}, f32[1024,64]{0,1:T(8,128)}, f32[1,64,1024]{2,0,1:T(1,128)}) async-done(((f32[64,1024]{1,0:T(8,128)}, f32[1024,64]{0,1:T(8,128)}, f32[1,64,1024]{2,0,1:T(1,128)}), (f32[64,1024]{1,0:T(8,128)}, f32[1024,64]{0,1:T(8,128)}, f32[1,64,1024]{2,0,1:T(1,128)})) %all-reduce.11.cloned.1.call-update) | async-done | bytes 786448 | tf_op jit(solution)/shard_map/psum | solution.py:116
  692.1 0.8 slice.80
  693.0 1.3 slice_subtract_fusion
  694.3 1.6 slice.79
  695.9 1.6 multiply_reduce_fusion
  698.2 1.6 multiply_reduce_fusion.1
  700.5 1.7 broadcast_divide_fusion.1
  702.2 0.3 pad_multiply_fusion
  702.5 1.7 broadcast_divide_fusion
  704.2 0.4 fusion.19
  704.8 0.7 fusion.21
  705.5 0.8 copy.24
  (39 shorter events, 1.0 us)
Async XLA Ops:
  7.2 60.4 %copy-start = (bf16[64,1024]{1,0:T(8,128)(2,1)S(1)}, bf16[64,1024]{1,0:T(8,128)(2,1)}, u32[]{:S(2)}) copy-start(bf16[64,1024]{1,0:T(8,128)(2,1)} %param.19) | copy-start | bytes 393220
  7.2 13.5 %copy-start.3 = (f32[1,64,1024]{2,1,0:T(8,128)S(1)}, f32[1,64,1024]{2,1,0:T(8,128)}, u32[]{:S(2)}) copy-start(f32[1,64,1024]{2,1,0:T(8,128)} %param.12) | copy-start | bytes 786436
  7.2 37.1 %copy-start.12 = (s32[5]{0:T(128)S(1)}, s32[5]{0:T(128)}, u32[]{:S(2)}) copy-start(s32[5]{0:T(128)} %param.16) | copy-start | bytes 64
  7.2 37.1 %copy-start.8 = (s32[1,1024]{1,0:T(1,128)S(1)}, s32[1,1024]{1,0:T(1,128)}, u32[]{:S(2)}) copy-start(s32[1,1024]{1,0:T(1,128)} %param.17) | copy-start | bytes 12292
  7.2 59.9 %copy-start.5 = (f32[1,64,64]{2,1,0:T(8,128)S(1)}, f32[1,64,64]{2,1,0:T(8,128)}, u32[]{:S(2)}) copy-start(f32[1,64,64]{2,1,0:T(8,128)} %param.15) | copy-start | bytes 49156
  7.2 60.3 %copy-start.10 = (f32[1024]{0:T(1024)S(1)}, f32[1024]{0:T(1024)}, u32[]{:S(2)}) copy-start(f32[1024]{0:T(1024)} %param.21) | copy-start | bytes 12292
  7.2 60.3 %copy-start.11 = (f32[1024]{0:T(1024)S(1)}, f32[1024]{0:T(1024)}, u32[]{:S(2)}) copy-start(f32[1024]{0:T(1024)} %param.20) | copy-start | bytes 12292
  25.9 41.3 %all-to-all-start = ((f32[1,64,1024]{2,0,1:T(1,128)}), f32[1,64,1024]{2,0,1:T(1,128)S(1)}, u32[]{:S(2)}, u32[]{:S(2)}) async-start(f32[1,64,1024]{2,0,1:T(1,128)} %fusion.18), calls=%async_computation | async-start | bytes 524288 | tf_op jit(solution)/shard_map/all_to_all | solution.py:80
  67.6 1.5 copy-start.6
  67.6 1.5 copy-start.7
  67.6 1.5 copy-start.9
  69.1 1.3 copy-start.1
  74.8 527.8 %all-to-all-start.1 = ((f32[64,1,1024]{2,1,0:T(1,128)}), f32[64,1,1024]{2,1,0:T(1,128)S(1)}, u32[]{:S(2)}, u32[]{:S(2)}) async-start(f32[64,1,1024]{2,1,0:T(1,128)} %copy.23), calls=%async_computation.1 | async-start | bytes 524288 | tf_op jit(solution)/shard_map/all_to_all | solution.py:117
  79.7 522.9 %all-reduce.9.cloned.1.call-start = ((), (), s32[]{:S(2)}) async-start(), calls=%async_computation.2 | async-start | bytes 1048576 | tf_op jit(solution)/shard_map/psum | solution.py:116
  83.7 608.4 %all-reduce.11.cloned.1.call-start = ((), (), s32[]{:S(2)}) async-start(), calls=%async_computation.3 | async-start | bytes 1572864 | tf_op jit(solution)/shard_map/psum | solution.py:116
  602.6 0.7 copy-start.4
  692.1 12.0 %copy-start.2 = (f32[1,64,1024]{2,0,1:T(1,128)S(1)}, f32[1,64,1024]{2,0,1:T(1,128)}, u32[]{:S(2)}) copy-start(f32[1,64,1024]{2,0,1:T(1,128)} %get-tuple-element.40) | copy-start | bytes 786436
Sparse Core Ops, SparseCore 0:
  84.0 518.5 all-reduce.8
  606.6 85.4 all-reduce.10

commit v2 on v0

--- a/solution.py
+++ b/solution.py
@@ -2,6 +2,11 @@
 import jax.numpy as jnp
 from jax import lax
 from jax.sharding import PartitionSpec as P
+
+
+def lay_frames(shard_in):
+    newest = jax.lax.all_gather(shard_in, axis_name="ens")
+    return jnp.sum(newest, axis=0)
 
 
 def noise(code, cell):
@@ -115,7 +120,7 @@
     g_in, g_out, back = lax.fori_loop(0, lat_local, per_row, start)
     g_in, g_out = lax.psum((g_in, g_out), ("ens", "slab"))
     returned = lax.all_to_all(back, "slab", split_axis=0, concat_axis=1, tiled=True)
-    summed = lax.psum(returned, "ens")
+    summed = lay_frames(returned)
     grad_state = diffuse(summed, east, north)
     return (normalized(g_in), normalized(g_out), grad_state)
 

time: 653 us -> 556 us (0.85)
  the two profiles are of different devices: /device:TPU:32 before, /device:TPU:2 now
where the time goes in v2:
time: 556 us
  waiting for transfers between devices  486 us (87%)
  starting transfers between devices  23.7 us (4%)
  between operations  17.9 us (3%)
  other arithmetic  12.6 us (2%)
  matrix products  9.94 us (2%)
  local copies, waits for them, and re-layouts  5.77 us (1%)
    psum x1, waiting for transfers between devices, on_device(): g_in, g_out = lax.psum((g_in, g_out), ('ens', 'slab'))  444 us
    all_to_all x1, waiting for transfers between devices, on_device(): lax.all_to_all(fresh, 'slab', split_axis=1, concat_axis=0, tiled=True)  22.7 us
    all_to_all x1, waiting for transfers between devices, on_device(): lax.all_to_all(back, 'slab', split_axis=0, concat_axis=1, tiled=True)  18.8 us
    all_to_all x1, starting transfers between devices, on_device(): lax.all_to_all(fresh, 'slab', split_axis=1, concat_axis=0, tiled=True)  18.7 us
  transfers between devices with their start and end apart: 4, of which 3 were waited for; matrix products, arithmetic and copies ran while one was open for 2% of the time, Pallas kernels for 0%

profile of v2, /device:TPU:2, one launch (start us, length us, event | category | flops | bytes accessed | tf_op | source)
XLA Modules:
  0.0 555.9 jit_solution(10946490092386185770)
XLA Ops:
  8.8 1.5 fusion.15
  10.3 0.1 slice.72
  10.5 1.7 convert_multiply_fusion.3
  12.2 0.1 slice.74
  12.2 1.6 fusion.17
  13.8 1.0 copy.24
  14.8 18.7 %all-to-all-start = ((f32[1,64,1024]{2,0,1:T(1,128)}), f32[1,64,1024]{2,0,1:T(1,128)S(1)}, u32[]{:S(2)}, u32[]{:S(2)}) async-start(f32[1,64,1024]{2,0,1:T(1,128)} %copy.24), calls=%async_computation | async-start | bytes 524288 | tf_op jit(solution)/shard_map/all_to_all | solution.py:85
  33.6 0.1 convert_reduce_fusion
  33.7 22.7 %all-to-all-done = f32[1,64,1024]{2,0,1:T(1,128)S(1)} async-done(((f32[1,64,1024]{2,0,1:T(1,128)}), f32[1,64,1024]{2,0,1:T(1,128)S(1)}, u32[]{:S(2)}, u32[]{:S(2)}) %all-to-all-start) | async-done | bytes 262176 | tf_op jit(solution)/shard_map/all_to_all | solution.py:85
  56.4 0.4 convolution_convert_fusion
  56.9 1.4 multiply_convert_fusion
  58.3 0.8 fusion.5
  59.1 0.5 copy-done.1
  59.6 2.1 fusion.1
  61.8 0.8 fusion.36
  62.5 0.5 convolution_bitcast_fusion
  63.0 1.0 copy.25
  64.0 4.9 all-to-all-start.1
  69.0 2.8 fusion.37
  71.8 1.2 fusion.35
  73.0 18.8 %all-to-all-done.1 = f32[64,1,1024]{2,1,0:T(1,128)S(1)} async-done(((f32[64,1,1024]{2,1,0:T(1,128)}), f32[64,1,1024]{2,1,0:T(1,128)S(1)}, u32[]{:S(2)}, u32[]{:S(2)}) %all-to-all-start.1) | async-done | bytes 262176 | tf_op jit(solution)/shard_map/all_to_all | solution.py:122
  91.8 0.7 copy-done.3
  92.5 444.4 %all-reduce.7.cloned.1.call-done = (f32[64,1024]{1,0:T(8,128)}, f32[1024,64]{0,1:T(8,128)}) async-done(((f32[64,1024]{1,0:T(8,128)}, f32[1024,64]{0,1:T(8,128)}), (f32[64,1024]{1,0:T(8,128)}, f32[1024,64]{0,1:T(8,128)})) %all-reduce.7.cloned.1.call-update) | async-done | bytes 524304 | tf_op jit(solution)/shard_map/psum | solution.py:121
  537.0 1.6 multiply_reduce_fusion
  539.3 1.6 multiply_reduce_fusion.1
  541.6 1.7 broadcast_divide_fusion.1
  543.3 1.7 broadcast_divide_fusion
  545.0 2.1 copy.27
  547.1 0.1 reduce.1
  547.3 0.1 slice.79
  547.4 0.1 convert_multiply_fusion.2
  547.6 0.8 fusion.19
  (35 shorter events, 0.4 us)
Async XLA Ops:
  8.0 48.8 %copy-start = (bf16[64,1024]{1,0:T(8,128)(2,1)S(1)}, bf16[64,1024]{1,0:T(8,128)(2,1)}, u32[]{:S(2)}) copy-start(bf16[64,1024]{1,0:T(8,128)(2,1)} %param.19) | copy-start | bytes 393220
  8.0 25.5 %copy-start.11 = (s32[5]{0:T(128)S(1)}, s32[5]{0:T(128)}, u32[]{:S(2)}) copy-start(s32[5]{0:T(128)} %param.16) | copy-start | bytes 64
  8.0 25.6 %copy-start.7 = (s32[1,1024]{1,0:T(1,128)S(1)}, s32[1,1024]{1,0:T(1,128)}, u32[]{:S(2)}) copy-start(s32[1,1024]{1,0:T(1,128)} %param.17) | copy-start | bytes 12292
  8.0 48.4 %copy-start.4 = (f32[1,64,64]{2,1,0:T(8,128)S(1)}, f32[1,64,64]{2,1,0:T(8,128)}, u32[]{:S(2)}) copy-start(f32[1,64,64]{2,1,0:T(8,128)} %param.15) | copy-start | bytes 49156
  8.0 48.8 %copy-start.9 = (f32[1024]{0:T(1024)S(1)}, f32[1024]{0:T(1024)}, u32[]{:S(2)}) copy-start(f32[1024]{0:T(1024)} %param.21) | copy-start | bytes 12292
  8.1 48.8 %copy-start.10 = (f32[1024]{0:T(1024)S(1)}, f32[1024]{0:T(1024)}, u32[]{:S(2)}) copy-start(f32[1024]{0:T(1024)} %param.20) | copy-start | bytes 12292
  14.8 41.6 %all-to-all-start = ((f32[1,64,1024]{2,0,1:T(1,128)}), f32[1,64,1024]{2,0,1:T(1,128)S(1)}, u32[]{:S(2)}, u32[]{:S(2)}) async-start(f32[1,64,1024]{2,0,1:T(1,128)} %copy.24), calls=%async_computation | async-start | bytes 524288 | tf_op jit(solution)/shard_map/all_to_all | solution.py:85
  56.8 1.5 copy-start.5
  56.9 1.5 copy-start.6
  56.9 1.5 copy-start.8
  58.3 1.3 copy-start.1
  64.0 27.8 %all-to-all-start.1 = ((f32[64,1,1024]{2,1,0:T(1,128)}), f32[64,1,1024]{2,1,0:T(1,128)S(1)}, u32[]{:S(2)}, u32[]{:S(2)}) async-start(f32[64,1,1024]{2,1,0:T(1,128)} %copy.25), calls=%async_computation.1 | async-start | bytes 524288 | tf_op jit(solution)/shard_map/all_to_all | solution.py:122
  68.9 468.0 %all-reduce.7.cloned.1.call-start = ((), (), s32[]{:S(2)}) async-start(), calls=%async_computation.3 | async-start | bytes 1048576 | tf_op jit(solution)/shard_map/psum | solution.py:121
  73.0 472.0 %all-gather.3.cloned.1.call-start = ((), (), s32[]{:S(2)}) async-start(), calls=%async_computation.2 | async-start | bytes 2359296 | tf_op jit(solution)/shard_map/all_gather | solution.py:8
  91.8 0.7 copy-start.3
  543.3 4.1 copy-start.2
Sparse Core Ops, SparseCore 0:
  75.8 461.0 all-reduce.6
Sparse Core Ops, SparseCore 1:
  92.6 37.7 all-gather.2
